TPU v7x, 512 devices: a whole 4x8x8 slice. The times are simulated.
512 devices in a mesh: grp: 8 (over y_lo, core), tile: 64 (over y_hi, x, z).
Axes of the slice: x: 4, y: 8 (y_hi: 2, y_lo: 4; y = y_hi * 4 + y_lo), z: 8, core: 2. Of those that a mesh axis runs over, the one named last changes fastest.
Arguments:
- hidden: bfloat16 [8, 512, 128, 128], P('grp', 'tile'), may hold values from -13 to 13
- cotangent: float32 [8, 512, 128], P('grp', 'tile'), may hold values from -16 to 16
- spectral_w: bfloat16 [4096, 256], P('tile'), may hold values from -0.375 to 0.375
- conv_k: float32 [9, 128], replicated, may hold values from -2 to 2
- proj_w: float32 [128], replicated, may hold values from -0.5 to 0.5
Outputs:
- grad_hidden: float32 [8, 512, 128, 128], P('grp', 'tile')
- grad_spectral: float32 [4096, 256], P('tile')
- grad_conv: float32 [9, 128], replicated
- grad_proj: float32 [128], replicated
All inputs are finite; a program needn't handle non-finite values.
Results may differ from a plain program's by a relative error of at most 0.015.
Values may be sent and summed in bfloat16 or wider, within the bound.
No kernel may reach another device: no remote copies, remote signals or barrier semaphores. Data moves between devices by JAX's collectives and lax.ppermute only.
A program may use at most 64 MiB of HBM per device.

v0:
```python
import jax
import jax.numpy as jnp
from jax import lax
from jax.sharding import PartitionSpec as P

HIGH = lax.Precision.HIGHEST


def padded(block, sides, width):
    for axis, dim in sides:
        count = lax.axis_size(axis)
        forward = [(i, i + 1) for i in range(count - 1)]
        backward = [(target, source) for source, target in forward]
        low = lax.ppermute(
            lax.slice_in_dim(block, block.shape[dim] - width, None, axis=dim), axis, forward
        )
        high = lax.ppermute(lax.slice_in_dim(block, 0, width, axis=dim), axis, backward)
        block = jnp.concatenate([low, block, high], axis=dim)
    return block


def spectral_tables(modes, bins):
    mode_idx = jnp.arange(modes, dtype=jnp.int32)
    bin_idx = jnp.arange(bins, dtype=jnp.int32)
    phase_int = mode_idx[:, None] * bin_idx[None, :] % bins
    angle_val = phase_int.astype(jnp.float32) * (2.0 * jnp.pi / bins)
    cosine = jnp.cos(angle_val)
    sine = jnp.sin(angle_val)
    forward_tab = jnp.concatenate([cosine, -sine], 0).astype(jnp.bfloat16)
    weight_k = jnp.where(mode_idx == 0, 1.0, 2.0).astype(jnp.float32)[:, None] / bins
    inverse_tab = jnp.concatenate([cosine * weight_k, -sine * weight_k], 0).T.astype(jnp.bfloat16)
    return (forward_tab, inverse_tab)


def build_mixer(weights, modes, chans):
    real_w = weights[:, :chans].reshape(modes, chans, chans)
    imag_w = weights[:, chans:].reshape(modes, chans, chans)
    upper = jnp.concatenate([real_w, imag_w], 2)
    lower = jnp.concatenate([-imag_w, real_w], 2)
    return jnp.concatenate([upper, lower], 1)


def gelu_pair(value):
    normal_cdf = 0.5 * (1.0 + jax.scipy.special.erf(value * 0.7071067811865476))
    return (
        value * normal_cdf,
        normal_cdf + value * jnp.exp(-0.5 * value * value) * 0.3989422804014327,
    )


def cell_backward(hidden_cells, local_term, cot_cells, mixer, forward_tab, inverse_tab, proj_w):
    modes = mixer.shape[0]
    chans = proj_w.shape[0]
    spec_h = jnp.einsum(
        "jb,pbc->jpc", forward_tab, hidden_cells, preferred_element_type=jnp.float32
    ).astype(jnp.bfloat16)
    h_cat = jnp.concatenate([spec_h[:modes], spec_h[modes:]], 2)
    mixed = jnp.einsum("kpa,kab->kpb", h_cat, mixer, preferred_element_type=jnp.float32).astype(
        jnp.bfloat16
    )
    mixed_stack = jnp.concatenate([mixed[:, :, :chans], mixed[:, :, chans:]], 0)
    spectral_out = jnp.einsum(
        "bj,jpo->pbo", inverse_tab, mixed_stack, preferred_element_type=jnp.float32
    )
    pre_act = spectral_out + local_term
    activ, slope = gelu_pair(pre_act)
    proj_grad = jnp.einsum("pb,pbo->o", cot_cells, activ, precision=HIGH)
    grad_pre = (cot_cells[:, :, None] * proj_w * slope).astype(jnp.bfloat16)
    grad_mix = jnp.einsum(
        "bj,pbo->jpo", inverse_tab, grad_pre, preferred_element_type=jnp.float32
    ).astype(jnp.bfloat16)
    grad_real = grad_mix[:modes]
    grad_imag = grad_mix[modes:]
    grad_cat = jnp.concatenate([grad_real, grad_imag], 2)
    grad_spec = jnp.einsum(
        "kpb,kab->kpa", grad_cat, mixer, preferred_element_type=jnp.float32
    ).astype(jnp.bfloat16)
    grad_stack = jnp.concatenate([grad_spec[:, :, :chans], grad_spec[:, :, chans:]], 0)
    grad_in = jnp.einsum("jb,jpc->pbc", forward_tab, grad_stack, preferred_element_type=jnp.float32)
    left_side = jnp.concatenate([spec_h[:modes], spec_h[modes:]], 1)
    right_side = jnp.concatenate([grad_cat, jnp.concatenate([grad_imag, -grad_real], 2)], 1)
    weight_term = jnp.einsum(
        "kpc,kpo->kco", left_side, right_side, preferred_element_type=jnp.float32
    ).reshape(modes * chans, 2 * chans)
    return (grad_pre, grad_in, weight_term, proj_grad)


def local(hidden, cotangent, spectral_w, conv_k, proj_w):
    rows_here, cols_here, bins_here, chans = hidden.shape
    modes = spectral_w.shape[0] * lax.axis_size("tile") // chans
    cell_count = rows_here * cols_here
    forward_tab, inverse_tab = spectral_tables(modes, bins_here)
    x_pad = padded(hidden, (("grp", 0), ("tile", 1)), 1)
    offsets = [(row_off, col_off) for row_off in (-1, 0, 1) for col_off in (-1, 0, 1)]
    local_term = jnp.zeros((rows_here, cols_here, bins_here, chans), jnp.float32)
    for index_d, (row_off, col_off) in enumerate(offsets):
        window = x_pad[1 + row_off : 1 + row_off + rows_here, 1 + col_off : 1 + col_off + cols_here]
        local_term = local_term + window.astype(jnp.float32) * conv_k[index_d]
    whole_w = lax.all_gather(spectral_w, "tile", axis=0, tiled=True)
    mixer = build_mixer(whole_w, modes, chans)
    grad_pre, grad_in, weight_term, proj_grad = cell_backward(
        hidden.reshape(cell_count, bins_here, chans),
        local_term.reshape(cell_count, bins_here, chans),
        cotangent.reshape(cell_count, bins_here),
        mixer,
        forward_tab,
        inverse_tab,
        proj_w,
    )
    grad_block = grad_pre.reshape(rows_here, cols_here, bins_here, chans)
    conv_part = jnp.stack(
        [
            jnp.einsum(
                "xybc,xybc->c",
                x_pad[1 + row_off : 1 + row_off + rows_here, 1 + col_off : 1 + col_off + cols_here],
                grad_block,
                preferred_element_type=jnp.float32,
            )
            for row_off, col_off in offsets
        ],
        0,
    )
    grad_pad = padded(grad_block, (("grp", 0), ("tile", 1)), 1)
    grad_hidden = grad_in.reshape(rows_here, cols_here, bins_here, chans)
    for index_d, (row_off, col_off) in enumerate(offsets):
        window = grad_pad[
            1 - row_off : 1 - row_off + rows_here, 1 - col_off : 1 - col_off + cols_here
        ]
        grad_hidden = grad_hidden + window.astype(jnp.float32) * conv_k[index_d]
    tile_share = lax.psum_scatter(weight_term, "tile", scatter_dimension=0, tiled=True)
    grad_spectral = lax.psum(tile_share.astype(jnp.bfloat16), "grp").astype(jnp.float32)
    conv_all, proj_all = lax.psum((conv_part, proj_grad), ("grp", "tile"))
    return (grad_hidden, grad_spectral, conv_all, proj_all)


def solution(mesh):
    in_specs = (P("grp", "tile", None, None), P("grp", "tile", None), P("tile", None), P(), P())
    out_specs = (P("grp", "tile", None, None), P("tile", None), P(), P())
    return jax.shard_map(local, mesh=mesh, in_specs=in_specs, out_specs=out_specs, check_vma=False)
```

profile of v0, /device:TPU:1, one launch (start us, length us, event | category | flops | bytes accessed | tf_op | source)
XLA Modules:
  0.0 639.4 jit_solution(11236863667525213482)
XLA Ops:
  7.9 1.1 copy.11
  9.1 8.8 %collective-permute-start.1 = (bf16[1,8,128,128]{2,3,1,0:T(8,128)(2,1)S(1)}, bf16[1,8,128,128]{2,3,1,0:T(8,128)(2,1)S(1)}, u32[]{:S(2)}, u32[]{:S(2)}) collective-permute-start(bf16[1,8,128,128]{2,3,1,0:T(8,128)(2,1)S(1)} %copy.11), channel_id=1, source_target_pairs={{64,0},{128,64},{192,128},{256,192},{320,256},{384,320},{448,384},... | collective-permute-start | bytes 786440 | tf_op jit(solution)/shard_map/ppermute | solution.py:17
  17.9 1.9 collective-permute-start
  19.9 1.1 convolution_convert_fusion.1
  21.1 1.0 slice_bitcast_fusion.8
  23.1 1.3 collective-permute-start.3
  24.4 4.0 collective-permute-start.2
  28.4 119.3 %all-gather.2.cloned.1.call-done = bf16[4096,256]{1,0:T(8,128)(2,1)} async-done(((bf16[64,256]{1,0:T(8,128)(2,1)}), bf16[4096,256]{1,0:T(8,128)(2,1)}) %all-gather.2.cloned.1.call-update) | async-done | bytes 2097168 | tf_op jit(solution)/shard_map/all_gather | solution.py:99
  147.7 1.7 fusion.52
  150.9 1.6 bitcast_convert_fusion
  152.8 2.7 fusion.24
  155.5 6.4 %collective-permute-start.5 = (bf16[1,8,128,128]{2,3,1,0:T(8,128)(2,1)S(1)}, bf16[1,8,128,128]{2,3,1,0:T(8,128)(2,1)}, u32[]{:S(2)}, u32[]{:S(2)}) collective-permute-start(bf16[1,8,128,128]{2,3,1,0:T(8,128)(2,1)S(1)} %bitcast.128), channel_id=1, source_target_pairs={{64,0},{128,64},{192,128},{256,192},{320,256},{384,320},{448,384},... | collective-permute-start | bytes 786440 | tf_op jit(solution)/shard_map/ppermute | solution.py:17
  161.9 5.1 collective-permute-start.4
  167.4 1.0 fusion.14
  168.4 1.2 fusion.15
  169.7 3.2 fusion.3
  173.5 97.4 %all-reduce = (f32[9,128]{1,0:T(8,128)}, f32[128]{0:T(128)}) all-reduce(f32[9,128]{1,0:T(8,128)S(1)} %stack.39, f32[128]{0:T(128)S(1)} %convolution_bitcast_fusion.2), channel_id=1, replica_groups=mesh['grp'=8,'tile'=64] {'grp','tile'}, use_global_device_ids=true, to_apply=%region_2.3 | all-reduce | flops 1280 | bytes 10240 | tf_op jit(solution)/shard_map/psum | solution.py:132
  271.8 1.3 collective-permute-start.6
  273.1 4.0 collective-permute-start.7
  277.5 1.3 collective-permute-done.7
  278.9 2.1 fusion.21
  281.1 1.0 copy.20
  282.1 273.8 %reduce-scatter.2.cloned.1.call-done = f32[64,256]{1,0:T(8,128)} async-done(((f32[4096,256]{1,0:T(8,128)}), f32[64,256]{1,0:T(8,128)}) %reduce-scatter.2.cloned.1.call-update) | async-done | bytes 65552 | tf_op jit(solution)/shard_map/reduce_scatter | solution.py:130
  556.7 75.3 %psum.21 = bf16[64,256]{1,0:T(8,128)(2,1)S(1)} all-reduce(bf16[64,256]{1,0:T(8,128)(2,1)S(1)} %convert_element_type.112), channel_id=1, replica_groups=mesh['grp'=8,'tile'=64] {'grp'}, use_global_device_ids=true, to_apply=%region_1.2 | all-reduce | flops 16384 | bytes 65536 | tf_op jit(solution)/shard_map/psum | solution.py:131
  (89 shorter events, 7.3 us)
Async XLA Ops:
  7.2 140.5 %all-gather.2.cloned.1.call-start = ((), (), s32[]{:S(2)}) async-start(), calls=%async_computation.1 | async-start | bytes 2129920 | tf_op jit(solution)/shard_map/all_gather | solution.py:99
  7.9 548.0 %reduce-scatter.2.cloned.1.call-start = ((), (), s32[]{:S(2)}) async-start(), calls=%async_computation.2 | async-start | bytes 4259840 | tf_op jit(solution)/shard_map/reduce_scatter | solution.py:130
  9.1 13.2 %collective-permute-start.1 = (bf16[1,8,128,128]{2,3,1,0:T(8,128)(2,1)S(1)}, bf16[1,8,128,128]{2,3,1,0:T(8,128)(2,1)S(1)}, u32[]{:S(2)}, u32[]{:S(2)}) collective-permute-start(bf16[1,8,128,128]{2,3,1,0:T(8,128)(2,1)S(1)} %copy.11), channel_id=1, source_target_pairs={{64,0},{128,64},{192,128},{256,192},{320,256},{384,320},{448,384},... | collective-permute-start | bytes 786440 | tf_op jit(solution)/shard_map/ppermute | solution.py:17
  17.9 5.2 collective-permute-start
  22.1 128.7 %copy-start.5 = (f32[128]{0:T(128)}, f32[128]{0:T(128)S(1)}, u32[]{:S(2)}) copy-start(f32[128]{0:T(128)S(1)} %get-tuple-element.35) | copy-start | bytes 1540
  22.1 128.7 %copy-start.7 = (f32[128]{0:T(128)}, f32[128]{0:T(128)S(1)}, u32[]{:S(2)}) copy-start(f32[128]{0:T(128)S(1)} %get-tuple-element.36) | copy-start | bytes 1540
  22.1 128.7 %copy-start.9 = (f32[128]{0:T(128)}, f32[128]{0:T(128)S(1)}, u32[]{:S(2)}) copy-start(f32[128]{0:T(128)S(1)} %get-tuple-element.37) | copy-start | bytes 1540
  22.1 128.7 %copy-start.11 = (f32[128]{0:T(128)}, f32[128]{0:T(128)S(1)}, u32[]{:S(2)}) copy-start(f32[128]{0:T(128)S(1)} %get-tuple-element.38) | copy-start | bytes 1540
  22.1 128.7 %copy-start.13 = (f32[128]{0:T(128)}, f32[128]{0:T(128)S(1)}, u32[]{:S(2)}) copy-start(f32[128]{0:T(128)S(1)} %get-tuple-element.39) | copy-start | bytes 1540
  22.1 128.7 %copy-start.15 = (f32[128]{0:T(128)}, f32[128]{0:T(128)S(1)}, u32[]{:S(2)}) copy-start(f32[128]{0:T(128)S(1)} %get-tuple-element.40) | copy-start | bytes 1540
  22.1 128.7 %copy-start.17 = (f32[128]{0:T(128)}, f32[128]{0:T(128)S(1)}, u32[]{:S(2)}) copy-start(f32[128]{0:T(128)S(1)} %get-tuple-element.41) | copy-start | bytes 1540
  22.1 128.7 %copy-start.19 = (f32[128]{0:T(128)}, f32[128]{0:T(128)S(1)}, u32[]{:S(2)}) copy-start(f32[128]{0:T(128)S(1)} %get-tuple-element.42) | copy-start | bytes 1540
  22.2 128.7 %copy-start.21 = (f32[128]{0:T(128)}, f32[128]{0:T(128)S(1)}, u32[]{:S(2)}) copy-start(f32[128]{0:T(128)S(1)} %get-tuple-element.43) | copy-start | bytes 1540
  23.1 127.7 %collective-permute-start.3 = (bf16[3,1,128,128]{2,3,1,0:T(8,128)(2,1)S(1)}, bf16[3,1,128,128]{2,3,1,0:T(8,128)(2,1)S(1)}, u32[]{:S(2)}, u32[]{:S(2)}) collective-permute-start(bf16[3,1,128,128]{2,3,1,0:T(8,128)(2,1)S(1)} %get-tuple-element.24), channel_id=1, source_target_pairs={{1,0},{2,1},{3,2},{4,3},{5,4},{6,5},{7,6},{8,7},{9,8},{10,9},{11,1... | collective-permute-start | bytes 294920 | tf_op jit(solution)/shard_map/ppermute | solution.py:17
  24.4 126.4 %collective-permute-start.2 = (bf16[3,1,128,128]{2,3,1,0:T(8,128)(2,1)S(1)}, bf16[3,1,128,128]{2,3,1,0:T(8,128)(2,1)S(1)}, u32[]{:S(2)}, u32[]{:S(2)}) collective-permute-start(bf16[3,1,128,128]{2,3,1,0:T(8,128)(2,1)S(1)} %get-tuple-element.25), channel_id=1, source_target_pairs={{0,1},{1,2},{2,3},{3,4},{4,5},{5,6},{6,7},{7,8},{8,9},{9,10},{10,1... | collective-permute-start | bytes 294920 | tf_op jit(solution)/shard_map/ppermute | solution.py:14
  155.5 115.4 %collective-permute-start.5 = (bf16[1,8,128,128]{2,3,1,0:T(8,128)(2,1)S(1)}, bf16[1,8,128,128]{2,3,1,0:T(8,128)(2,1)}, u32[]{:S(2)}, u32[]{:S(2)}) collective-permute-start(bf16[1,8,128,128]{2,3,1,0:T(8,128)(2,1)S(1)} %bitcast.128), channel_id=1, source_target_pairs={{64,0},{128,64},{192,128},{256,192},{320,256},{384,320},{448,384},... | collective-permute-start | bytes 786440 | tf_op jit(solution)/shard_map/ppermute | solution.py:17
  161.9 109.0 %collective-permute-start.4 = (bf16[1,8,128,128]{2,3,1,0:T(8,128)(2,1)S(1)}, bf16[1,8,128,128]{2,3,1,0:T(8,128)(2,1)}, u32[]{:S(2)}, u32[]{:S(2)}) collective-permute-start(bf16[1,8,128,128]{2,3,1,0:T(8,128)(2,1)S(1)} %bitcast.129), channel_id=1, source_target_pairs={{0,64},{64,128},{128,192},{192,256},{256,320},{320,384},{384,448},... | collective-permute-start | bytes 786440 | tf_op jit(solution)/shard_map/ppermute | solution.py:14
  169.6 109.2 %copy-start.6 = (f32[128]{0:T(128)S(1)}, f32[128]{0:T(128)}, u32[]{:S(2)}) copy-start(f32[128]{0:T(128)} %copy-done.5) | copy-start | bytes 1540
  169.6 109.2 %copy-start.8 = (f32[128]{0:T(128)S(1)}, f32[128]{0:T(128)}, u32[]{:S(2)}) copy-start(f32[128]{0:T(128)} %copy-done.7) | copy-start | bytes 1540
  169.6 109.2 %copy-start.10 = (f32[128]{0:T(128)S(1)}, f32[128]{0:T(128)}, u32[]{:S(2)}) copy-start(f32[128]{0:T(128)} %copy-done.9) | copy-start | bytes 1540
  169.6 109.2 %copy-start.12 = (f32[128]{0:T(128)S(1)}, f32[128]{0:T(128)}, u32[]{:S(2)}) copy-start(f32[128]{0:T(128)} %copy-done.11) | copy-start | bytes 1540
  169.7 109.2 %copy-start.14 = (f32[128]{0:T(128)S(1)}, f32[128]{0:T(128)}, u32[]{:S(2)}) copy-start(f32[128]{0:T(128)} %copy-done.13) | copy-start | bytes 1540
  271.8 5.8 collective-permute-start.6
  273.1 5.8 collective-permute-start.7
  (13 other events, 466.0 us)
Sparse Core Ops, SparseCore 0:
  12.6 135.0 all-gather.1
  155.6 400.1 reduce-scatter.1
where the time goes:
time: 640 us; the launch traced here: 639 us
  waiting for transfers between devices  396 us (62%)
  blocking collectives  173 us (27%)
  starting transfers between devices  32.8 us (5%)
  between operations  14.6 us (2%)
  matrix products  12.4 us (2%)
    reduce_scatter x1, waiting for transfers between devices, local(): lax.psum_scatter(weight_term, 'tile', scatter_dimension=0, tiled=True)  274 us
    all_gather x1, waiting for transfers between devices, local(): whole_w = lax.all_gather(spectral_w, 'tile', axis=0, tiled=True)  119 us
    psum x1, blocking collectives, local(): conv_all, proj_all = lax.psum((conv_part, proj_grad), ('grp', 'tile'))  97.4 us
    psum x1, blocking collectives, local(): lax.psum(tile_share.astype(jnp.bfloat16), 'grp').astype(jnp.float32)  75.3 us
    ppermute x4, starting transfers between devices, padded(): lax.ppermute(lax.slice_in_dim(block, 0, width, axis=dim), axis, backward)  17.8 us
    ppermute x4, starting transfers between devices, padded(): lax.ppermute(lax.slice_in_dim(block, block.shape[dim] - width, None, axis...  15 us
  transfers between devices with their start and end apart: 10, of which 5 were waited for; matrix products, arithmetic and copies ran while one was open for 3% of the time, Pallas kernels for 0%

commit v1 on v0

--- a/solution.py
+++ b/solution.py
@@ -4,6 +4,11 @@
 from jax.sharding import PartitionSpec as P
 
 HIGH = lax.Precision.HIGHEST
+
+
+def axis_by_axis(value_2, inner_axis, outer_axis):
+    half = lax.psum(value_2, inner_axis)
+    return lax.psum(half, outer_axis)
 
 
 def padded(block, sides, width):
@@ -129,7 +134,7 @@
         grad_hidden = grad_hidden + window.astype(jnp.float32) * conv_k[index_d]
     tile_share = lax.psum_scatter(weight_term, "tile", scatter_dimension=0, tiled=True)
     grad_spectral = lax.psum(tile_share.astype(jnp.bfloat16), "grp").astype(jnp.float32)
-    conv_all, proj_all = lax.psum((conv_part, proj_grad), ("grp", "tile"))
+    conv_all, proj_all = axis_by_axis((conv_part, proj_grad), "grp", "tile")
     return (grad_hidden, grad_spectral, conv_all, proj_all)
 
 

time: 640 us -> 641 us (level)
  blocking collectives: 173 us -> 282 us
  waiting for transfers between devices: 396 us -> 288 us
    psum x1 -> x2, blocking collectives: 97.4 us -> 209 us  [the longest x1 197 us: axis_by_axis(): return lax.psum(half, outer_axis)]
    reduce_scatter x1, waiting for transfers between devices: 274 us -> 166 us  [local(): lax.psum_scatter(weight_term, 'tile', scatter_dimension=0, tiled=True)]
where the time goes in v1:
time: 641 us; the launch traced here: 640 us
  waiting for transfers between devices  288 us (45%)
  blocking collectives  282 us (44%)
  starting transfers between devices  32.8 us (5%)
  between operations  14.7 us (2%)
  matrix products  12.3 us (2%)
    psum x1, blocking collectives, axis_by_axis(): return lax.psum(half, outer_axis)  197 us
    reduce_scatter x1, waiting for transfers between devices, local(): lax.psum_scatter(weight_term, 'tile', scatter_dimension=0, tiled=True)  166 us
    all_gather x1, waiting for transfers between devices, local(): whole_w = lax.all_gather(spectral_w, 'tile', axis=0, tiled=True)  119 us
    psum x1, blocking collectives, local(): lax.psum(tile_share.astype(jnp.bfloat16), 'grp').astype(jnp.float32)  72.5 us
    ppermute x4, starting transfers between devices, padded(): lax.ppermute(lax.slice_in_dim(block, 0, width, axis=dim), axis, backward)  17.8 us
    ppermute x4, starting transfers between devices, padded(): lax.ppermute(lax.slice_in_dim(block, block.shape[dim] - width, None, axis...  15 us
  transfers between devices with their start and end apart: 10, of which 5 were waited for; matrix products, arithmetic and copies ran while one was open for 3% of the time, Pallas kernels for 0%

profile of v1, /device:TPU:1, one launch (start us, length us, event | category | flops | bytes accessed | tf_op | source)
XLA Modules:
  0.0 640.0 jit_solution(3420835751443176134)
XLA Ops:
  7.9 1.1 copy.11
  9.1 8.8 %collective-permute-start.1 = (bf16[1,8,128,128]{2,3,1,0:T(8,128)(2,1)S(1)}, bf16[1,8,128,128]{2,3,1,0:T(8,128)(2,1)S(1)}, u32[]{:S(2)}, u32[]{:S(2)}) collective-permute-start(bf16[1,8,128,128]{2,3,1,0:T(8,128)(2,1)S(1)} %copy.11), channel_id=1, source_target_pairs={{64,0},{128,64},{192,128},{256,192},{320,256},{384,320},{448,384},... | collective-permute-start | bytes 786440 | tf_op jit(solution)/shard_map/ppermute | solution.py:22
  17.9 1.9 collective-permute-start
  19.9 1.1 convolution_convert_fusion.1
  23.1 1.3 collective-permute-start.3
  24.4 4.0 collective-permute-start.2
  28.4 119.3 %all-gather.2.cloned.1.call-done = bf16[4096,256]{1,0:T(8,128)(2,1)} async-done(((bf16[64,256]{1,0:T(8,128)(2,1)}), bf16[4096,256]{1,0:T(8,128)(2,1)}) %all-gather.2.cloned.1.call-update) | async-done | bytes 2097168 | tf_op jit(solution)/shard_map/all_gather | solution.py:104
  147.7 1.7 fusion.52
  150.9 1.6 bitcast_convert_fusion
  152.8 2.7 fusion.24
  155.5 6.4 %collective-permute-start.5 = (bf16[1,8,128,128]{2,3,1,0:T(8,128)(2,1)S(1)}, bf16[1,8,128,128]{2,3,1,0:T(8,128)(2,1)}, u32[]{:S(2)}, u32[]{:S(2)}) collective-permute-start(bf16[1,8,128,128]{2,3,1,0:T(8,128)(2,1)S(1)} %bitcast.128), channel_id=1, source_target_pairs={{64,0},{128,64},{192,128},{256,192},{320,256},{384,320},{448,384},... | collective-permute-start | bytes 786440 | tf_op jit(solution)/shard_map/ppermute | solution.py:22
  161.9 5.1 collective-permute-start.4
  167.4 1.0 fusion.14
  168.4 1.2 fusion.15
  169.7 3.2 fusion.3
  173.5 11.8 %all-reduce.1 = (f32[9,128]{1,0:T(8,128)S(1)}, f32[128]{0:T(128)S(1)}) all-reduce(f32[9,128]{1,0:T(8,128)S(1)} %stack.39, f32[128]{0:T(128)S(1)} %convolution_bitcast_fusion.2), channel_id=1, replica_groups=mesh['grp'=8,'tile'=64] {'grp'}, use_global_device_ids=true, to_apply=%region_2.3 | all-reduce | flops 1280 | bytes 10240 | tf_op jit(solution)/shard_map/psum | solution.py:10
  185.3 197.2 %all-reduce = (f32[9,128]{1,0:T(8,128)}, f32[128]{0:T(128)}) all-reduce(f32[9,128]{1,0:T(8,128)S(1)} %get-tuple-element.18, f32[128]{0:T(128)S(1)} %get-tuple-element.19), channel_id=1, replica_groups=mesh['grp'=8,'tile'=64] {'tile'}, use_global_device_ids=true, to_apply=%region_3.4 | all-reduce | flops 1280 | bytes 10240 | tf_op jit(solution)/shard_map/psum | solution.py:11
  383.4 1.3 collective-permute-start.6
  384.7 4.0 collective-permute-start.7
  389.2 1.3 collective-permute-done.7
  390.5 2.1 fusion.21
  392.6 1.0 copy.20
  393.6 165.5 %reduce-scatter.2.cloned.1.call-done = f32[64,256]{1,0:T(8,128)} async-done(((f32[4096,256]{1,0:T(8,128)}), f32[64,256]{1,0:T(8,128)}) %reduce-scatter.2.cloned.1.call-update) | async-done | bytes 65552 | tf_op jit(solution)/shard_map/reduce_scatter | solution.py:135
  560.0 72.5 %psum.35 = bf16[64,256]{1,0:T(8,128)(2,1)S(1)} all-reduce(bf16[64,256]{1,0:T(8,128)(2,1)S(1)} %convert_element_type.112), channel_id=1, replica_groups=mesh['grp'=8,'tile'=64] {'grp'}, use_global_device_ids=true, to_apply=%region_1.2 | all-reduce | flops 16384 | bytes 65536 | tf_op jit(solution)/shard_map/psum | solution.py:136
  (90 shorter events, 8.3 us)
Async XLA Ops:
  7.2 140.5 %all-gather.2.cloned.1.call-start = ((), (), s32[]{:S(2)}) async-start(), calls=%async_computation.1 | async-start | bytes 2129920 | tf_op jit(solution)/shard_map/all_gather | solution.py:104
  7.9 551.2 %reduce-scatter.2.cloned.1.call-start = ((), (), s32[]{:S(2)}) async-start(), calls=%async_computation.2 | async-start | bytes 4259840 | tf_op jit(solution)/shard_map/reduce_scatter | solution.py:135
  9.1 13.2 %collective-permute-start.1 = (bf16[1,8,128,128]{2,3,1,0:T(8,128)(2,1)S(1)}, bf16[1,8,128,128]{2,3,1,0:T(8,128)(2,1)S(1)}, u32[]{:S(2)}, u32[]{:S(2)}) collective-permute-start(bf16[1,8,128,128]{2,3,1,0:T(8,128)(2,1)S(1)} %copy.11), channel_id=1, source_target_pairs={{64,0},{128,64},{192,128},{256,192},{320,256},{384,320},{448,384},... | collective-permute-start | bytes 786440 | tf_op jit(solution)/shard_map/ppermute | solution.py:22
  17.9 5.2 collective-permute-start
  22.1 128.7 %copy-start.7 = (f32[128]{0:T(128)}, f32[128]{0:T(128)S(1)}, u32[]{:S(2)}) copy-start(f32[128]{0:T(128)S(1)} %get-tuple-element.38) | copy-start | bytes 1540
  22.1 128.7 %copy-start.9 = (f32[128]{0:T(128)}, f32[128]{0:T(128)S(1)}, u32[]{:S(2)}) copy-start(f32[128]{0:T(128)S(1)} %get-tuple-element.39) | copy-start | bytes 1540
  22.1 128.7 %copy-start.11 = (f32[128]{0:T(128)}, f32[128]{0:T(128)S(1)}, u32[]{:S(2)}) copy-start(f32[128]{0:T(128)S(1)} %get-tuple-element.40) | copy-start | bytes 1540
  22.1 128.7 %copy-start.13 = (f32[128]{0:T(128)}, f32[128]{0:T(128)S(1)}, u32[]{:S(2)}) copy-start(f32[128]{0:T(128)S(1)} %get-tuple-element.41) | copy-start | bytes 1540
  22.1 128.7 %copy-start.15 = (f32[128]{0:T(128)}, f32[128]{0:T(128)S(1)}, u32[]{:S(2)}) copy-start(f32[128]{0:T(128)S(1)} %get-tuple-element.42) | copy-start | bytes 1540
  23.1 127.6 %collective-permute-start.3 = (bf16[3,1,128,128]{2,3,1,0:T(8,128)(2,1)S(1)}, bf16[3,1,128,128]{2,3,1,0:T(8,128)(2,1)S(1)}, u32[]{:S(2)}, u32[]{:S(2)}) collective-permute-start(bf16[3,1,128,128]{2,3,1,0:T(8,128)(2,1)S(1)} %get-tuple-element.26), channel_id=1, source_target_pairs={{1,0},{2,1},{3,2},{4,3},{5,4},{6,5},{7,6},{8,7},{9,8},{10,9},{11,1... | collective-permute-start | bytes 294920 | tf_op jit(solution)/shard_map/ppermute | solution.py:22
  24.4 126.4 %collective-permute-start.2 = (bf16[3,1,128,128]{2,3,1,0:T(8,128)(2,1)S(1)}, bf16[3,1,128,128]{2,3,1,0:T(8,128)(2,1)S(1)}, u32[]{:S(2)}, u32[]{:S(2)}) collective-permute-start(bf16[3,1,128,128]{2,3,1,0:T(8,128)(2,1)S(1)} %get-tuple-element.27), channel_id=1, source_target_pairs={{0,1},{1,2},{2,3},{3,4},{4,5},{5,6},{6,7},{7,8},{8,9},{9,10},{10,1... | collective-permute-start | bytes 294920 | tf_op jit(solution)/shard_map/ppermute | solution.py:19
  155.5 227.1 %collective-permute-start.5 = (bf16[1,8,128,128]{2,3,1,0:T(8,128)(2,1)S(1)}, bf16[1,8,128,128]{2,3,1,0:T(8,128)(2,1)}, u32[]{:S(2)}, u32[]{:S(2)}) collective-permute-start(bf16[1,8,128,128]{2,3,1,0:T(8,128)(2,1)S(1)} %bitcast.128), channel_id=1, source_target_pairs={{64,0},{128,64},{192,128},{256,192},{320,256},{384,320},{448,384},... | collective-permute-start | bytes 786440 | tf_op jit(solution)/shard_map/ppermute | solution.py:22
  161.9 220.7 %collective-permute-start.4 = (bf16[1,8,128,128]{2,3,1,0:T(8,128)(2,1)S(1)}, bf16[1,8,128,128]{2,3,1,0:T(8,128)(2,1)}, u32[]{:S(2)}, u32[]{:S(2)}) collective-permute-start(bf16[1,8,128,128]{2,3,1,0:T(8,128)(2,1)S(1)} %bitcast.129), channel_id=1, source_target_pairs={{0,64},{64,128},{128,192},{192,256},{256,320},{320,384},{384,448},... | collective-permute-start | bytes 786440 | tf_op jit(solution)/shard_map/ppermute | solution.py:19
  169.6 220.9 %copy-start.6 = (f32[128]{0:T(128)S(1)}, f32[128]{0:T(128)}, u32[]{:S(2)}) copy-start(f32[128]{0:T(128)} %copy-done.5) | copy-start | bytes 1540
  169.6 220.8 %copy-start.8 = (f32[128]{0:T(128)S(1)}, f32[128]{0:T(128)}, u32[]{:S(2)}) copy-start(f32[128]{0:T(128)} %copy-done.7) | copy-start | bytes 1540
  169.6 220.8 %copy-start.10 = (f32[128]{0:T(128)S(1)}, f32[128]{0:T(128)}, u32[]{:S(2)}) copy-start(f32[128]{0:T(128)} %copy-done.9) | copy-start | bytes 1540
  169.6 220.8 %copy-start.12 = (f32[128]{0:T(128)S(1)}, f32[128]{0:T(128)}, u32[]{:S(2)}) copy-start(f32[128]{0:T(128)} %copy-done.11) | copy-start | bytes 1540
  169.7 220.8 %copy-start.14 = (f32[128]{0:T(128)S(1)}, f32[128]{0:T(128)}, u32[]{:S(2)}) copy-start(f32[128]{0:T(128)} %copy-done.13) | copy-start | bytes 1540
  169.7 220.8 %copy-start.16 = (f32[128]{0:T(128)S(1)}, f32[128]{0:T(128)}, u32[]{:S(2)}) copy-start(f32[128]{0:T(128)} %copy-done.15) | copy-start | bytes 1540
  169.7 220.8 %copy-start.18 = (f32[128]{0:T(128)S(1)}, f32[128]{0:T(128)}, u32[]{:S(2)}) copy-start(f32[128]{0:T(128)} %copy-done.17) | copy-start | bytes 1540
  169.7 220.8 %copy-start.20 = (f32[128]{0:T(128)S(1)}, f32[128]{0:T(128)}, u32[]{:S(2)}) copy-start(f32[128]{0:T(128)} %copy-done.19) | copy-start | bytes 1540
  169.7 220.8 %copy-start.22 = (f32[128]{0:T(128)S(1)}, f32[128]{0:T(128)}, u32[]{:S(2)}) copy-start(f32[128]{0:T(128)} %copy-done.21) | copy-start | bytes 1540
  383.4 5.8 collective-permute-start.6
  384.7 5.7 collective-permute-start.7
  (13 other events, 544.0 us)
Sparse Core Ops, SparseCore 0:
  12.6 135.0 all-gather.1
  155.7 403.4 reduce-scatter.1
